TPU v7x, 512 devices: a whole 4x4x16 slice. The times are simulated.
512 devices in a mesh: ep: 64 (over y, z_lo, core), dp: 8 (over z_hi, x).
Axes of the slice: x: 4, y: 4, z: 16 (z_hi: 2, z_lo: 8; z = z_hi * 8 + z_lo), core: 2. Of those that a mesh axis runs over, the one named last changes fastest.
Arguments:
- hidden: bfloat16 [2, 16384, 2048], P(None, ('ep', 'dp')), may hold values from -6 to 6
- norm_gain: bfloat16 [2048], replicated, may hold values from 0.5 to 1.5
- gate_weights: float32 [2, 16384, 8], P(None, ('ep', 'dp')), may hold values from 0.05 to 1
- routes: int32 [2, 16384, 8], P(None, ('ep', 'dp')), may hold values from 0 to 63, as said below
- replica_pick: int32 [2, 16384, 8], P(None, ('ep', 'dp')), may hold values from 0 to 4095
- trainer_experts: int32 [64], replicated, may hold values from 0 to 63, each once
- hot_experts: int32 [3], replicated, may hold values from 0 to 63, as said below
- replica_hot: int32 [64], replicated, may hold values from 0 to 2, as said below
- w_gate: bfloat16 [64, 2048, 384], P('ep', 'dp'), may hold values from -0.125 to 0.125
- w_up: bfloat16 [64, 2048, 384], P('ep', 'dp'), may hold values from -0.125 to 0.125
- w_down: bfloat16 [64, 384, 2048], P('ep', None, 'dp'), may hold values from -0.3125 to 0.3125
- queries: bfloat16 [2, 16384, 4096], P(None, ('ep', 'dp')), may hold values from -6 to 6
- key_cache: bfloat16 [16384, 32, 512], P(('ep', 'dp')), may hold values from -6 to 6
- value_cache: bfloat16 [16384, 32, 512], P(('ep', 'dp')), may hold values from -6 to 6
- new_keys: bfloat16 [2, 16384, 512], P(None, ('ep', 'dp')), may hold values from -6 to 6
- new_values: bfloat16 [2, 16384, 512], P(None, ('ep', 'dp')), may hold values from -6 to 6
- cache_lengths: int32 [16384], P(('ep', 'dp')), may hold values from 2 to 32, as said below
Outputs:
- mixed: bfloat16 [2, 16384, 2048], P(None, ('ep', 'dp'))
- context: bfloat16 [2, 16384, 4096], P(None, ('ep', 'dp'))
Inputs may be any that keep to these rules, and one draw needn't show every extreme that they name: Trainer index p holds expert trainer_experts[p]; each expert once. `hot_experts`: 3 different experts, among them expert 0 and expert 64 - 1. `replica_hot`: every entry of hot_experts is named by some index. `cache_lengths`: the 32 sequences of each device include one with 32 live entries. `routes`: each row names 8 different experts; every expert is named by some row.
All inputs are finite; a program needn't handle non-finite values.
Results may differ from a plain program's by a relative error of at most 0.001.
The roundings to bfloat16 on the way count: a program that leaves them out, or rounds other values in their place, can miss the bound.
Values may be sent and summed in bfloat16 or wider, within the bound.
A program may use at most 64 MiB of HBM per device.

v0:
```python
import math
import jax
import jax.numpy as jnp
from jax import lax
from jax.sharding import PartitionSpec as P

HEADS = 32
KV_HEADS = 4
HEAD = 128
TOP = 8
CAP = 3
SLOTS = 2
norm_epsilon = 1e-06


def spread(shard, axis, root):
    mine = lax.axis_index(axis) == root
    return lax.psum(jnp.where(mine, shard, jnp.zeros_like(shard)), axis)


def scaled_norm(hidden_rows, norm_gain):
    values = hidden_rows.astype(jnp.float32)
    mean_square = jnp.mean(values * values, axis=-1, keepdims=True)
    return (values * lax.rsqrt(mean_square + norm_epsilon) * norm_gain.astype(jnp.float32)).astype(
        jnp.bfloat16
    )


def table_lookup(onehot_rows, table):
    return jnp.dot(onehot_rows, table, preferred_element_type=jnp.int32)


def attend(query_rows, key_cache, value_cache, new_keys, new_values, cache_lengths, step_index):
    rows_here = query_rows.shape[0]
    cache_len = key_cache.shape[1]
    steps_all = new_keys.shape[0]
    grouped = query_rows.reshape(rows_here, KV_HEADS, HEADS // KV_HEADS, HEAD)
    keys_cached = key_cache.reshape(rows_here, cache_len, KV_HEADS, HEAD)
    values_cached = value_cache.reshape(rows_here, cache_len, KV_HEADS, HEAD)
    keys_fresh = new_keys.reshape(steps_all, rows_here, KV_HEADS, HEAD)
    values_fresh = new_values.reshape(steps_all, rows_here, KV_HEADS, HEAD)
    score_scale = 1.0 / math.sqrt(HEAD)
    cache_scores = (
        jnp.einsum("rkgh,rckh->rkgc", grouped, keys_cached, preferred_element_type=jnp.float32)
        * score_scale
    )
    fresh_scores = (
        jnp.einsum("rkgh,srkh->rkgs", grouped, keys_fresh, preferred_element_type=jnp.float32)
        * score_scale
    )
    cache_mask = (jnp.arange(cache_len, dtype=jnp.int32)[None, :] < cache_lengths[:, None])[
        :, None, None, :
    ]
    fresh_mask = (jnp.arange(steps_all, dtype=jnp.int32) <= step_index)[None, None, None, :]
    row_max = jnp.maximum(
        jnp.max(jnp.where(cache_mask, cache_scores, -1e30), axis=-1),
        jnp.max(jnp.where(fresh_mask, fresh_scores, -1e30), axis=-1),
    )
    cache_exp = jnp.where(cache_mask, jnp.exp(cache_scores - row_max[..., None]), 0.0)
    fresh_exp = jnp.where(fresh_mask, jnp.exp(fresh_scores - row_max[..., None]), 0.0)
    row_total = jnp.sum(cache_exp, axis=-1) + jnp.sum(fresh_exp, axis=-1)
    cache_probs = (cache_exp / row_total[..., None]).astype(jnp.bfloat16)
    fresh_probs = (fresh_exp / row_total[..., None]).astype(jnp.bfloat16)
    summed = jnp.einsum(
        "rkgc,rckh->rkgh", cache_probs, values_cached, preferred_element_type=jnp.float32
    )
    summed = summed + jnp.einsum(
        "rkgs,srkh->rkgh", fresh_probs, values_fresh, preferred_element_type=jnp.float32
    )
    return summed.astype(jnp.bfloat16).reshape(rows_here, HEADS * HEAD)


def body(
    hidden,
    norm_gain,
    gate_weights,
    routes,
    replica_pick,
    trainer_experts,
    hot_experts,
    replica_hot,
    w_gate,
    w_up,
    w_down,
    queries,
    key_cache,
    value_cache,
    new_keys,
    new_values,
    cache_lengths,
):
    ep_count = lax.axis_size("ep")
    my_device = lax.axis_index("ep")
    device_ids = jnp.arange(ep_count, dtype=jnp.int32)
    expert_count = trainer_experts.shape[0]
    expert_ids = jnp.arange(expert_count, dtype=jnp.int32)
    hot_count = hot_experts.shape[0]
    hot_ids = jnp.arange(hot_count, dtype=jnp.int32)
    home_device = jnp.sum(
        jnp.where(trainer_experts[None, :] == expert_ids[:, None], device_ids[None, :], 0), axis=1
    )
    hosted = jnp.sum(
        jnp.where(replica_hot[:, None] == hot_ids[None, :], hot_experts[None, :], 0), axis=1
    )
    is_replica = (hosted[None, :] == expert_ids[:, None]).astype(jnp.int32)
    replica_order = jnp.cumsum(is_replica, axis=1) * is_replica
    copies = 1 + jnp.sum(is_replica, axis=1)
    my_hot = jnp.sum(jnp.where(device_ids == my_device, replica_hot, 0))
    own_pair = jnp.concatenate([w_gate, w_up], axis=0)
    replica_pair = jnp.zeros_like(own_pair)
    replica_down = jnp.zeros_like(w_down)
    for hot_index in range(hot_count):
        hot_expert = jnp.sum(jnp.where(hot_ids == hot_index, hot_experts, 0))
        root_device = jnp.sum(jnp.where(expert_ids == hot_expert, home_device, 0))
        sent_pair, sent_down = (
            spread(own_pair, "ep", root_device),
            spread(w_down, "ep", root_device),
        )
        wanted = my_hot == hot_index
        replica_pair = jnp.where(wanted, sent_pair, replica_pair)
        replica_down = jnp.where(wanted, sent_down, replica_down)
    slot_pair, slot_down = (
        lax.all_gather(jnp.stack([own_pair, replica_pair]), "dp", axis=2, tiled=True),
        lax.all_gather(jnp.concatenate([w_down, replica_down], axis=0), "dp", axis=2, tiled=True),
    )
    tokens_here = hidden.shape[1]
    width = hidden.shape[2]
    entries = tokens_here * TOP
    slot_total = ep_count * SLOTS
    buffer_rows = slot_total * CAP
    entry_ids = jnp.arange(entries, dtype=jnp.int32)
    token_map = (
        (entry_ids // TOP)[:, None] == jnp.arange(tokens_here, dtype=jnp.int32)[None, :]
    ).astype(jnp.float32)
    contract_first = (((0,), (0,)), ((), ()))
    mixed_steps = []
    context_steps = []
    for step_index in range(hidden.shape[0]):
        context_steps.append(
            attend(
                queries[step_index],
                key_cache,
                value_cache,
                new_keys,
                new_values,
                cache_lengths,
                step_index,
            )
        )
        normed = scaled_norm(hidden[step_index], norm_gain)
        weights_top = gate_weights[step_index]
        gates = (weights_top / jnp.sum(weights_top, axis=-1, keepdims=True)).astype(jnp.bfloat16)
        chosen = routes[step_index].reshape(entries)
        replica_picks = replica_pick[step_index].reshape(entries)
        expert_onehot = (chosen[:, None] == expert_ids[None, :]).astype(jnp.int32)
        replica_index = replica_picks % table_lookup(expert_onehot, copies)
        order_rows = table_lookup(expert_onehot, replica_order)
        replica_device = jnp.sum(
            jnp.where(order_rows == replica_index[:, None], device_ids[None, :], 0), axis=1
        )
        target = jnp.where(
            replica_index == 0, table_lookup(expert_onehot, home_device), replica_device
        )
        second_slot = (replica_index > 0).astype(jnp.int32)
        slot_index = target * SLOTS + second_slot
        slot_onehot = (
            slot_index[:, None] == jnp.arange(slot_total, dtype=jnp.int32)[None, :]
        ).astype(jnp.int32)
        slot_rank = jnp.sum(jnp.cumsum(slot_onehot, axis=0) * slot_onehot, axis=1) - 1
        is_kept = slot_rank < CAP
        row_index = second_slot * (ep_count * CAP) + target * CAP + slot_rank
        placed = (
            is_kept[:, None]
            & (row_index[:, None] == jnp.arange(buffer_rows, dtype=jnp.int32)[None, :])
        ).astype(jnp.float32)
        dispatch = lax.dot_general(placed, token_map, contract_first).astype(jnp.bfloat16)
        weighted = placed * gates.reshape(entries).astype(jnp.float32)[:, None]
        combine_map = lax.dot_general(token_map, weighted, contract_first).astype(jnp.bfloat16)
        outgoing = jnp.dot(dispatch, normed, preferred_element_type=jnp.float32).astype(
            jnp.bfloat16
        )
        outgoing = outgoing.reshape(SLOTS, ep_count, CAP, width)
        incoming = lax.all_to_all(outgoing, "ep", split_axis=1, concat_axis=1, tiled=True)
        slot_rows = incoming.reshape(SLOTS, ep_count * CAP, width)
        projected = jnp.einsum(
            "snd,skdf->sknf", slot_rows, slot_pair, preferred_element_type=jnp.float32
        )
        hidden_units = (jax.nn.silu(projected[:, 0]) * projected[:, 1]).astype(jnp.bfloat16)
        expert_out = jnp.einsum(
            "snf,sfd->snd", hidden_units, slot_down, preferred_element_type=jnp.float32
        ).astype(jnp.bfloat16)
        expert_out = expert_out.reshape(SLOTS, ep_count, CAP, width)
        returned = lax.all_to_all(
            expert_out, "ep", split_axis=1, concat_axis=1, tiled=True
        ).reshape(buffer_rows, width)
        mixed_rows = hidden[step_index].astype(jnp.float32) + jnp.dot(
            combine_map, returned, preferred_element_type=jnp.float32
        )
        mixed_steps.append(mixed_rows.astype(jnp.bfloat16))
    return (jnp.stack(mixed_steps), jnp.stack(context_steps))


def solution(mesh):
    return jax.shard_map(
        body,
        mesh=mesh,
        in_specs=(
            P(None, ("ep", "dp"), None),
            P(),
            P(None, ("ep", "dp"), None),
            P(None, ("ep", "dp"), None),
            P(None, ("ep", "dp"), None),
            P(),
            P(),
            P(),
            P("ep", "dp", None),
            P("ep", "dp", None),
            P("ep", None, "dp"),
            P(None, ("ep", "dp"), None),
            P(("ep", "dp"), None, None),
            P(("ep", "dp"), None, None),
            P(None, ("ep", "dp"), None),
            P(None, ("ep", "dp"), None),
            P(("ep", "dp")),
        ),
        out_specs=(P(None, ("ep", "dp"), None), P(None, ("ep", "dp"), None)),
        check_vma=False,
    )
```

profile of v0, /device:TPU:1, one launch (start us, length us, event | category | flops | bytes accessed | tf_op | source)
XLA Modules:
  0.0 1533.9 jit_solution(9489303480555903428)
XLA Ops:
  8.1 1.4 fusion.152
  9.5 2.7 fusion.153
  16.0 1.8 broadcast_select_fusion.3
  21.1 825.0 %all-reduce.3.cloned.1.call-done = (bf16[1,384,256]{2,1,0:T(8,128)(2,1)}, bf16[1,384,256]{2,1,0:T(8,128)(2,1)}, bf16[1,384,256]{2,1,0:T(8,128)(2,1)}, bf16[2,256...) async-done(((bf16[1,384,256]{2,1,0:T(8,128)(2,1)}, bf16[1,384,256]{2,1,0:T(8,128)(2,1)}, bf16[1,384,256]{2,1,0:T(8,128)(2,1)}, ...) | async-done | bytes 1769488 | tf_op jit(solution)/shard_map/psum | solution.py:18
  846.1 1.1 select_bitcast_fusion
  851.0 2.1 convolution_convert_fusion.2
  853.0 4.0 reshape.209
  857.0 3.2 copy.100
  860.2 11.6 all-to-all-start.2
  873.8 2.1 convolution_convert_fusion.3
  875.9 4.0 reshape.204
  879.9 3.2 copy.90
  883.1 93.7 %all-to-all-done.2 = bf16[2,64,3,2048]{3,0,2,1:T(2,128)(2,1)} async-done(((bf16[2,64,3,2048]{3,0,2,1:T(2,128)(2,1)}), bf16[2,64,3,2048]{3,0,2,1:T(2,128)(2,1)}, u32[]{:S(2)}, u32[]{:S(2)}) %all-to-all-start.2) | async-done | bytes 1572896 | tf_op jit(solution)/shard_map/all_to_all | solution.py:183
  976.8 6.8 all-to-all-start
  985.6 128.7 %all-gather.3.cloned.1.call-done = bf16[2,2,2048,384]{3,2,1,0:T(8,128)(2,1)} async-done(((bf16[2,2,256,384]{3,2,1,0:T(8,128)(2,1)}), bf16[2,2,2048,384]{3,2,1,0:T(8,128)(2,1)}) %all-gather.3.cloned.1.call-update) | async-done | bytes 6291472 | tf_op jit(solution)/shard_map/all_gather | solution.py:123
  1114.3 6.1 fusion.13
  1120.5 224.6 %all-gather.5.cloned.1.call-done = bf16[2,384,2048]{2,1,0:T(8,128)(2,1)} async-done(((bf16[2,384,256]{2,1,0:T(8,128)(2,1)}), bf16[2,384,2048]{2,1,0:T(8,128)(2,1)}) %all-gather.5.cloned.1.call-update) | async-done | bytes 3145744 | tf_op jit(solution)/shard_map/all_gather | solution.py:124
  1345.1 3.3 convolution_convert_fusion
  1348.3 2.8 copy.103
  1351.1 1.1 copy-done.3
  1352.3 9.7 all-to-all-start.3
  1362.0 5.2 fusion.10
  1368.2 2.8 copy.93
  1370.9 64.5 %all-to-all-done.3 = bf16[2,64,3,2048]{3,0,2,1:T(2,128)(2,1)S(1)} async-done(((bf16[2,64,3,2048]{3,0,2,1:T(2,128)(2,1)}), bf16[2,64,3,2048]{3,0,2,1:T(2,128)(2,1)S(1)}, u32[]{:S(2)}, u32[]{:S(2)}) %all-to-all-start.3) | async-done | bytes 1572896 | tf_op jit(solution)/shard_map/all_to_all | solution.py:193
  1435.5 1.1 copy-done.1
  1436.6 8.6 all-to-all-start.1
  1457.8 2.5 copy.104
  1460.3 2.5 reshape.212
  1462.8 55.9 %all-to-all-done.1 = bf16[2,64,3,2048]{3,0,2,1:T(2,128)(2,1)} async-done(((bf16[2,64,3,2048]{3,0,2,1:T(2,128)(2,1)}), bf16[2,64,3,2048]{3,0,2,1:T(2,128)(2,1)}, u32[]{:S(2)}, u32[]{:S(2)}) %all-to-all-start.1) | async-done | bytes 1572896 | tf_op jit(solution)/shard_map/all_to_all | solution.py:193
  1518.6 2.5 copy.94
  1521.2 2.5 reshape.207
  1523.7 2.2 fusion.4
  (164 shorter events, 26.8 us)
Async XLA Ops:
  7.2 1447.5 %copy-start = (bf16[32,32,512]{2,1,0:T(8,128)(2,1)S(1)}, bf16[32,32,512]{2,1,0:T(8,128)(2,1)}, u32[]{:S(2)}) copy-start(bf16[32,32,512]{2,1,0:T(8,128)(2,1)} %param.30) | copy-start | bytes 3145732
  7.2 838.9 %all-reduce.3.cloned.1.call-start = ((), (), s32[]{:S(2)}) async-start(), calls=%async_computation.6 | async-start | bytes 3538944 | tf_op jit(solution)/shard_map/psum | solution.py:18
  17.7 1.1 copy-start.30
  18.8 1095.6 %all-gather.3.cloned.1.call-start = ((), (), s32[]{:S(2)}) async-start(), calls=%async_computation.4 | async-start | bytes 7077888 | tf_op jit(solution)/shard_map/all_gather | solution.py:123
  847.2 1.1 copy-start.15
  847.2 1.3 copy-start.16
  847.2 1.5 copy-start.26
  847.2 3.3 copy-start.17
  847.2 3.5 copy-start.4
  850.9 6.1 copy-start.22
  860.2 116.5 %all-to-all-start.2 = ((bf16[2,64,3,2048]{3,0,2,1:T(2,128)(2,1)}), bf16[2,64,3,2048]{3,0,2,1:T(2,128)(2,1)}, u32[]{:S(2)}, u32[]{:S(2)}) async-start(bf16[2,64,3,2048]{3,0,2,1:T(2,128)(2,1)} %copy.100), calls=%async_computation.2 | async-start | bytes 3145728 | tf_op jit(solution)/shard_map/all_to_all | solution.py:183
  873.7 6.2 copy-start.24
  883.1 101.7 %copy-start.6 = (bf16[1,384,256]{2,1,0:T(8,128)(2,1)S(1)}, bf16[1,384,256]{2,1,0:T(8,128)(2,1)}, u32[]{:S(2)}) copy-start(bf16[1,384,256]{2,1,0:T(8,128)(2,1)} %param.27) | copy-start | bytes 589828
  976.8 374.4 %all-to-all-start = ((bf16[2,64,3,2048]{3,0,2,1:T(2,128)(2,1)}), bf16[2,64,3,2048]{3,0,2,1:T(2,128)(2,1)S(1)}, u32[]{:S(2)}, u32[]{:S(2)}) async-start(bf16[2,64,3,2048]{3,0,2,1:T(2,128)(2,1)} %copy.90), calls=%async_computation | async-start | bytes 3145728 | tf_op jit(solution)/shard_map/all_to_all | solution.py:183
  983.6 361.5 %all-gather.5.cloned.1.call-start = ((), (), s32[]{:S(2)}) async-start(), calls=%async_computation.5 | async-start | bytes 3538944 | tf_op jit(solution)/shard_map/all_gather | solution.py:124
  1351.1 1.1 copy-start.3
  1352.3 83.2 %all-to-all-start.3 = ((bf16[2,64,3,2048]{3,0,2,1:T(2,128)(2,1)}), bf16[2,64,3,2048]{3,0,2,1:T(2,128)(2,1)S(1)}, u32[]{:S(2)}, u32[]{:S(2)}) async-start(bf16[2,64,3,2048]{3,0,2,1:T(2,128)(2,1)} %bitcast.156), calls=%async_computation.3 | async-start | bytes 3145728 | tf_op jit(solution)/shard_map/all_to_all | solution.py:193
  1362.0 5.2 copy-start.29
  1435.5 1.1 copy-start.1
  1435.5 13.4 copy-start.7
  1436.6 82.0 %all-to-all-start.1 = ((bf16[2,64,3,2048]{3,0,2,1:T(2,128)(2,1)}), bf16[2,64,3,2048]{3,0,2,1:T(2,128)(2,1)}, u32[]{:S(2)}, u32[]{:S(2)}) async-start(bf16[2,64,3,2048]{3,0,2,1:T(2,128)(2,1)} %bitcast.155), calls=%async_computation.1 | async-start | bytes 3145728 | tf_op jit(solution)/shard_map/all_to_all | solution.py:193
  1445.2 3.8 copy-start.11
  1445.2 3.9 copy-start.12
  1448.9 2.0 copy-start.5
  1449.7 3.5 copy-start.27
  1451.6 1.5 copy-start.8
  1452.1 2.1 copy-start.13
  1454.7 0.9 copy-start.14
  1455.2 1.1 copy-start.9
  1521.2 2.5 copy-start.23
  1523.7 2.2 copy-start.2
  1523.7 2.2 copy-start.25
  (6 other events, 4.3 us)
Sparse Core Ops, SparseCore 0:
  18.9 827.1 all-reduce.2
  849.7 264.5 all-gather.2
  1118.4 226.5 all-gather.4
where the time goes:
time: 1540 us; the launch traced here: 1530 us
  waiting for transfers between devices  1390 us (90%)
  local copies, waits for them, and re-layouts  39.7 us (3%)
  starting transfers between devices  37 us (2%)
  matrix products  28.6 us (2%)
  other arithmetic  18.2 us (1%)
  between operations  18 us (1%)
    psum x1, waiting for transfers between devices, spread(): return lax.psum(jnp.where(mine, shard, jnp.zeros_like(shard)), axis)  825 us
    all_gather x1, waiting for transfers between devices, body(): lax.all_gather(jnp.concatenate([w_down, replica_down], axis=0), 'dp', axi...  225 us
    all_gather x1, waiting for transfers between devices, body(): lax.all_gather(jnp.stack([own_pair, replica_pair]), 'dp', axis=2, tiled=T...  129 us
    all_to_all x2, waiting for transfers between devices, body(): lax.all_to_all(expert_out, 'ep', split_axis=1, concat_axis=1, tiled=True)  120 us
    all_to_all x2, waiting for transfers between devices, body(): lax.all_to_all(outgoing, 'ep', split_axis=1, concat_axis=1, tiled=True)  93.7 us
  transfers between devices with their start and end apart: 7, of which 6 were waited for; matrix products, arithmetic and copies ran while one was open for 4% of the time, Pallas kernels for 0%

commit v1 on v0

--- a/solution.py
+++ b/solution.py
@@ -180,7 +180,10 @@
             jnp.bfloat16
         )
         outgoing = outgoing.reshape(SLOTS, ep_count, CAP, width)
-        incoming = lax.all_to_all(outgoing, "ep", split_axis=1, concat_axis=1, tiled=True)
+        incoming = jnp.concatenate(
+            lax.all_to_all(jnp.stack(jnp.split(outgoing, lax.axis_size("ep"), axis=1)), "ep", 0, 0),
+            axis=1,
+        )
         slot_rows = incoming.reshape(SLOTS, ep_count * CAP, width)
         projected = jnp.einsum(
             "snd,skdf->sknf", slot_rows, slot_pair, preferred_element_type=jnp.float32

time: 1540 us -> 1490 us (0.968)
  waiting for transfers between devices: 1390 us -> 1300 us
  local copies, waits for them, and re-layouts: 39.7 us -> 79.3 us
    all_gather x1, waiting for transfers between devices: 129 us -> 246 us  [body(): lax.all_gather(jnp.stack([own_pair, replica_pair]), 'dp', axis=2, tiled=T...]
    all_to_all x2, waiting for transfers between devices: 93.7 us -> 0.01 us  [body(): lax.all_to_all(jnp.stack(jnp.split(outgoing, lax.axis_size('ep'), axis=1)...]
    all_gather x1, waiting for transfers between devices: 225 us -> 143 us  [body(): lax.all_gather(jnp.concatenate([w_down, replica_down], axis=0), 'dp', axi...]
    psum x1, waiting for transfers between devices: 825 us -> 785 us  [spread(): return lax.psum(jnp.where(mine, shard, jnp.zeros_like(shard)), axis)]
    unnamed x68 -> x208, local copies, waits for them, and re-layouts: 4.01 us -> 41.9 us
  transfers between devices with their start and end apart: 7 -> 7, of which waited for: 6 -> 5; matrix products, arithmetic and copies ran while one was open for 4% -> 6% of each run, Pallas kernels for 0% -> 0%
where the time goes in v1:
time: 1490 us
  waiting for transfers between devices  1300 us (87%)
  local copies, waits for them, and re-layouts  79.3 us (5%)
  starting transfers between devices  47.8 us (3%)
  matrix products  30.5 us (2%)
  between operations  18.9 us (1%)
  other arithmetic  17.8 us (1%)
    psum x1, waiting for transfers between devices, spread(): return lax.psum(jnp.where(mine, shard, jnp.zeros_like(shard)), axis)  785 us
    all_gather x1, waiting for transfers between devices, body(): lax.all_gather(jnp.stack([own_pair, replica_pair]), 'dp', axis=2, tiled=T...  246 us
    all_gather x1, waiting for transfers between devices, body(): lax.all_gather(jnp.concatenate([w_down, replica_down], axis=0), 'dp', axi...  143 us
    all_to_all x2, waiting for transfers between devices, body(): lax.all_to_all(expert_out, 'ep', split_axis=1, concat_axis=1, tiled=True)  123 us
    unnamed x208, local copies, waits for them, and re-layouts  41.9 us
  transfers between devices with their start and end apart: 7, of which 5 were waited for; matrix products, arithmetic and copies ran while one was open for 6% of the time, Pallas kernels for 0%

profile of v1, /device:TPU:1, one launch (start us, length us, event | category | flops | bytes accessed | tf_op | source)
XLA Modules:
  0.0 1491.8 jit_solution(10073631238668534866)
XLA Ops:
  8.2 1.3 fusion.178
  13.4 1.1 fusion.56
  15.8 3.0 convolution_convert_fusion.3
  18.8 4.0 reshape.204
  24.4 3.2 copy.533
  27.6 17.5 %all-to-all-start = ((bf16[64,2,1,3,2048]{4,1,3,2,0:T(2,128)(2,1)}), bf16[64,2,1,3,2048]{4,1,3,2,0:T(2,128)(2,1)}, u32[]{:S(2)}, u32[]{:S(2)}) async-start(bf16[64,2,1,3,2048]{4,1,3,2,0:T(2,128)(2,1)} %copy.533), calls=%async_computation | async-start | bytes 3145728 | tf_op jit(solution)/shard_map/all_to_all | solution.py:184
  45.9 2.6 fusion.153
  50.7 1.0 broadcast_select_fusion
  57.7 2.1 convolution_convert_fusion.2
  59.7 4.0 reshape.209
  88.3 785.4 %all-reduce.3.cloned.1.call-done = (bf16[1,384,256]{2,1,0:T(8,128)(2,1)}, bf16[1,384,256]{2,1,0:T(8,128)(2,1)}, bf16[1,384,256]{2,1,0:T(8,128)(2,1)}, bf16[2,256...) async-done(((bf16[1,384,256]{2,1,0:T(8,128)(2,1)}, bf16[1,384,256]{2,1,0:T(8,128)(2,1)}, bf16[1,384,256]{2,1,0:T(8,128)(2,1)}, ...) | async-done | bytes 1769488 | tf_op jit(solution)/shard_map/psum | solution.py:18
  873.7 1.1 select_bitcast_fusion
  890.6 4.9 copy.606
  895.4 11.5 all-to-all-start.2
  907.9 245.7 %all-gather.3.cloned.1.call-done = bf16[2,2,2048,384]{3,2,1,0:T(8,128)(2,1)} async-done(((bf16[2,2,256,384]{3,2,1,0:T(8,128)(2,1)}), bf16[2,2,2048,384]{3,2,1,0:T(8,128)(2,1)}) %all-gather.3.cloned.1.call-update) | async-done | bytes 6291472 | tf_op jit(solution)/shard_map/all_gather | solution.py:123
  1153.6 6.0 fusion.10
  1159.7 143.0 %all-gather.5.cloned.1.call-done = bf16[2,384,2048]{2,1,0:T(8,128)(2,1)} async-done(((bf16[2,384,256]{2,1,0:T(8,128)(2,1)}), bf16[2,384,2048]{2,1,0:T(8,128)(2,1)}) %all-gather.5.cloned.1.call-update) | async-done | bytes 3145744 | tf_op jit(solution)/shard_map/all_gather | solution.py:124
  1302.7 3.3 convolution_convert_fusion.1
  1305.9 2.8 copy.536
  1308.7 1.1 copy-done.4
  1309.8 9.7 all-to-all-start.1
  1319.6 5.1 fusion.13
  1325.7 2.8 copy.609
  1328.5 64.5 %all-to-all-done.1 = bf16[2,64,3,2048]{3,0,2,1:T(2,128)(2,1)S(1)} async-done(((bf16[2,64,3,2048]{3,0,2,1:T(2,128)(2,1)}), bf16[2,64,3,2048]{3,0,2,1:T(2,128)(2,1)S(1)}, u32[]{:S(2)}, u32[]{:S(2)}) %all-to-all-start.1) | async-done | bytes 1572896 | tf_op jit(solution)/shard_map/all_to_all | solution.py:196
  1393.0 8.7 all-to-all-start.3
  1411.2 2.5 copy.537
  1413.7 2.5 reshape.207
  1416.3 58.9 %all-to-all-done.3 = bf16[2,64,3,2048]{3,0,2,1:T(2,128)(2,1)} async-done(((bf16[2,64,3,2048]{3,0,2,1:T(2,128)(2,1)}), bf16[2,64,3,2048]{3,0,2,1:T(2,128)(2,1)}, u32[]{:S(2)}, u32[]{:S(2)}) %all-to-all-start.3) | async-done | bytes 1572896 | tf_op jit(solution)/shard_map/all_to_all | solution.py:196
  1475.2 2.5 copy.610
  1477.8 2.5 reshape.212
  1480.3 2.1 fusion.5
  1482.4 2.1 fusion.4
  (306 shorter events, 64.2 us)
Async XLA Ops:
  7.2 1401.4 %copy-start = (bf16[32,32,512]{2,1,0:T(8,128)(2,1)S(1)}, bf16[32,32,512]{2,1,0:T(8,128)(2,1)}, u32[]{:S(2)}) copy-start(bf16[32,32,512]{2,1,0:T(8,128)(2,1)} %param.30) | copy-start | bytes 3145732
  8.0 4.5 copy-start.29
  8.1 3.6 copy-start.36
  11.3 34.7 %copy-start.31 = (s32[64]{0:T(128)}, s32[64]{0:T(128)S(1)}, u32[]{:S(2)}) copy-start(s32[64]{0:T(128)S(1)} %select_reduce_fusion.4) | copy-start | bytes 772
  27.6 17.6 %copy-start.33 = (s32[3]{0:T(128)S(1)}, s32[3]{0:T(128)}, u32[]{:S(2)}) copy-start(s32[3]{0:T(128)} %param.23) | copy-start | bytes 40
  27.6 22.9 %copy-start.9 = (bf16[1,256,384]{2,1,0:T(8,128)(2,1)S(1)}, bf16[1,256,384]{2,1,0:T(8,128)(2,1)}, u32[]{:S(2)}) copy-start(bf16[1,256,384]{2,1,0:T(8,128)(2,1)} %param.25) | copy-start | bytes 589828
  27.6 23.0 %copy-start.10 = (bf16[1,256,384]{2,1,0:T(8,128)(2,1)S(1)}, bf16[1,256,384]{2,1,0:T(8,128)(2,1)}, u32[]{:S(2)}) copy-start(bf16[1,256,384]{2,1,0:T(8,128)(2,1)} %param.26) | copy-start | bytes 589828
  27.6 24.1 %copy-start.6 = (bf16[1,384,256]{2,1,0:T(8,128)(2,1)S(1)}, bf16[1,384,256]{2,1,0:T(8,128)(2,1)}, u32[]{:S(2)}) copy-start(bf16[1,384,256]{2,1,0:T(8,128)(2,1)} %param.27) | copy-start | bytes 589828
  27.6 867.8 %all-to-all-start = ((bf16[64,2,1,3,2048]{4,1,3,2,0:T(2,128)(2,1)}), bf16[64,2,1,3,2048]{4,1,3,2,0:T(2,128)(2,1)}, u32[]{:S(2)}, u32[]{:S(2)}) async-start(bf16[64,2,1,3,2048]{4,1,3,2,0:T(2,128)(2,1)} %copy.533), calls=%async_computation | async-start | bytes 3145728 | tf_op jit(solution)/shard_map/all_to_all | solution.py:184
  45.2 828.6 %all-reduce.3.cloned.1.call-start = ((), (), s32[]{:S(2)}) async-start(), calls=%async_computation.6 | async-start | bytes 3538944 | tf_op jit(solution)/shard_map/psum | solution.py:18
  50.7 3.1 copy-start.37
  50.7 3.3 copy-start.32
  50.7 3.9 copy-start.17
  50.7 3.9 copy-start.30
  51.8 5.9 copy-start.2
  51.8 5.9 copy-start.24
  52.6 1101.0 %all-gather.3.cloned.1.call-start = ((), (), s32[]{:S(2)}) async-start(), calls=%async_computation.4 | async-start | bytes 7077888 | tf_op jit(solution)/shard_map/all_gather | solution.py:123
  895.4 11.6 copy-start.11
  895.4 11.6 copy-start.12
  895.4 11.6 copy-start.13
  895.4 11.7 copy-start.7
  895.4 413.3 %all-to-all-start.2 = ((bf16[64,2,1,3,2048]{4,1,3,2,0:T(2,128)(2,1)}), bf16[64,2,1,3,2048]{4,1,3,2,0:T(2,128)(2,1)S(1)}, u32[]{:S(2)}, u32[]{:S(2)}) async-start(bf16[64,2,1,3,2048]{4,1,3,2,0:T(2,128)(2,1)} %copy.606), calls=%async_computation.2 | async-start | bytes 3145728 | tf_op jit(solution)/shard_map/all_to_all | solution.py:184
  907.0 395.7 %all-gather.5.cloned.1.call-start = ((), (), s32[]{:S(2)}) async-start(), calls=%async_computation.5 | async-start | bytes 3538944 | tf_op jit(solution)/shard_map/all_gather | solution.py:124
  1309.8 83.2 %all-to-all-start.1 = ((bf16[2,64,3,2048]{3,0,2,1:T(2,128)(2,1)}), bf16[2,64,3,2048]{3,0,2,1:T(2,128)(2,1)S(1)}, u32[]{:S(2)}, u32[]{:S(2)}) async-start(bf16[2,64,3,2048]{3,0,2,1:T(2,128)(2,1)} %bitcast.924), calls=%async_computation.1 | async-start | bytes 3145728 | tf_op jit(solution)/shard_map/all_to_all | solution.py:196
  1319.5 5.2 copy-start.34
  1328.5 73.3 %copy-start.21 = (f32[2,32,8]{1,2,0:T(8,128)S(1)}, f32[2,32,8]{1,2,0:T(8,128)}, u32[]{:S(2)}) copy-start(f32[2,32,8]{1,2,0:T(8,128)} %param.19) | copy-start | bytes 6148
  1328.5 75.1 %copy-start.8 = (bf16[2,32,4096]{2,1,0:T(8,128)(2,1)S(1)}, bf16[2,32,4096]{2,1,0:T(8,128)(2,1)}, u32[]{:S(2)}) copy-start(bf16[2,32,4096]{2,1,0:T(8,128)(2,1)} %param.28) | copy-start | bytes 1572868
  1393.0 10.6 copy-start.1
  1393.0 10.7 copy-start.14
  1393.0 10.8 copy-start.15
  1393.0 82.2 %all-to-all-start.3 = ((bf16[2,64,3,2048]{3,0,2,1:T(2,128)(2,1)}), bf16[2,64,3,2048]{3,0,2,1:T(2,128)(2,1)}, u32[]{:S(2)}, u32[]{:S(2)}) async-start(bf16[2,64,3,2048]{3,0,2,1:T(2,128)(2,1)} %bitcast.923), calls=%async_computation.3 | async-start | bytes 3145728 | tf_op jit(solution)/shard_map/all_to_all | solution.py:196
  1477.8 4.7 copy-start.28
  (13 other events, 24.3 us)
Sparse Core Ops, SparseCore 0:
  52.7 820.9 all-reduce.2
  877.3 276.2 all-gather.2
  1157.7 144.8 all-gather.4
